TPU v7x, 32 devices: a whole 2x2x4 slice. The times are simulated.
32 devices in a mesh: groups: 2 (over y), dp: 4 (over z), tensor: 4 (over x, core).
Axes of the slice: x: 2, y: 2, z: 4, core: 2. Of those that a mesh axis runs over, the one named last changes fastest.
Arguments:
- hidden: bfloat16 [4096, 7168], P(('groups', 'dp'), 'tensor'), parts along dimension 0, may hold values from -6 to 6
- out_grad: bfloat16 [4096, 4096], P(('groups', 'dp'), 'tensor'), parts along dimension 0, may hold values from -6 to 6
- down_weight: bfloat16 [7168, 4096], P('tensor', 'dp'), may hold values from -0.09375 to 0.09375
- proj_in: bfloat16 [7168, 64], P('tensor'), may hold values from -0.0625 to 0.0625
- proj_out: bfloat16 [4096, 64], replicated, may hold values from -0.09375 to 0.09375
- queries: bfloat16 [4096, 4096], P('dp', 'tensor'), may hold values from -0.005859375 to 0.005859375
Outputs:
- hidden_grad: bfloat16 [4096, 7168], P(('groups', 'dp'), 'tensor'), parts along dimension 0
- scores: float32 [16, 4096], P(('groups', 'dp'), 'tensor'), parts along dimension 0
There are 2 independent parts, one for each index of `groups`. A program takes and returns all parts, laid end to end along the dimension named above; an argument that names none is the same for every part. Nothing has to cross between parts.
All inputs are finite; a program needn't handle non-finite values.
Results may differ from a plain program's by a relative error of at most 0.0028.
Values may be sent and summed in bfloat16 or wider, within the bound.
A program may use at most 128 MiB of HBM per device.

v0:
```python
import jax
import jax.numpy as jnp
from jax import lax
from jax.sharding import PartitionSpec as P

SEQ = 256


def local(hidden, out_grad, down_weight, proj_in, proj_out, queries):
    full_grad = lax.all_gather(out_grad, "tensor", axis=1, tiled=True)
    tok_rows = full_grad.shape[0]
    summed = lax.dot_general(
        full_grad,
        lax.all_gather(down_weight, "dp", axis=1, tiled=True),
        (((1,), (1,)), ((), ())),
        preferred_element_type=jnp.float32,
    )
    hidden_grad = summed.astype(jnp.bfloat16)
    rank = proj_in.shape[1]
    examples_here = tok_rows // SEQ
    slice_rows = rank // lax.axis_size("tensor")
    left = jnp.dot(hidden, proj_in, preferred_element_type=jnp.float32)
    right = jnp.dot(full_grad, proj_out, preferred_element_type=jnp.float32)
    right = right.reshape(examples_here, SEQ, rank)
    paired = lax.psum(left.reshape(tok_rows // 2, 2 * rank), "tensor")
    left_full = paired.reshape(examples_here, SEQ, rank)
    outer = jnp.einsum("esa,esb->eab", left_full, right, precision=lax.Precision.HIGHEST)
    outer = lax.dynamic_slice_in_dim(outer, lax.axis_index("tensor") * slice_rows, slice_rows, 1)
    features = outer.reshape(examples_here, slice_rows * rank).astype(jnp.bfloat16)
    everyone = lax.all_gather(features, "dp", axis=0, tiled=True)
    local_scores = lax.dot_general(
        everyone, queries, (((1,), (1,)), ((), ())), preferred_element_type=jnp.float32
    )
    partial_scores = lax.all_to_all(local_scores, "dp", split_axis=0, concat_axis=1, tiled=True)
    scores = lax.psum_scatter(partial_scores, "tensor", scatter_dimension=1, tiled=True)
    return (hidden_grad, scores)


def solution(mesh):
    in_specs = (
        P(("groups", "dp"), "tensor"),
        P(("groups", "dp"), "tensor"),
        P("tensor", "dp"),
        P("tensor", None),
        P(),
        P("dp", "tensor"),
    )
    out_specs = (P(("groups", "dp"), "tensor"), P(("groups", "dp"), "tensor"))
    return jax.shard_map(local, mesh=mesh, in_specs=in_specs, out_specs=out_specs, check_vma=False)
```

profile of v0, /device:TPU:0, one launch (start us, length us, event | category | flops | bytes accessed | tf_op | source)
XLA Modules:
  0.0 382.3 jit_solution(9735488778490877013)
XLA Ops:
  8.0 0.0 copy-start
  8.0 0.0 copy-start.1
  8.0 0.0 all-gather.4.cloned.1.call-start
  8.1 0.7 all-gather.4.cloned.1.call-update
  8.8 0.0 all-reduce.2.cloned.1.call-start
  8.8 2.2 fusion.3
  11.0 0.7 copy.23
  11.6 0.0 all-reduce.2.cloned.1.call-update
  11.7 0.0 reduce-scatter.4.cloned.1.call-start
  11.7 35.9 %all-gather.4.cloned.1.call-done = bf16[512,4096]{1,0:T(8,128)(2,1)} async-done(((bf16[512,1024]{1,0:T(8,128)(2,1)}), bf16[512,4096]{1,0:T(8,128)(2,1)}) %all-gather.4.cloned.1.call-update) | async-done | bytes 4194320 | tf_op jit(solution)/shard_map/all_gather | solution.py:10
  47.6 0.0 copy-done.1
  47.6 3.6 fusion.4
  51.2 30.7 %all-reduce.2.cloned.1.call-done = f32[2,256,64]{1,2,0:T(8,128)} async-done(((f32[2,256,64]{1,2,0:T(8,128)}), f32[2,256,64]{1,2,0:T(8,128)}) %all-reduce.2.cloned.1.call-update) | async-done | bytes 131088 | tf_op jit(solution)/shard_map/psum | solution.py:25
  82.0 1.2 fusion
  83.1 0.1 reshape.22
  83.2 13.2 %all-gather = bf16[4,2,1024]{2,1,0:T(2,128)(2,1)S(1)} all-gather(bf16[1,2,1024]{2,1,0:T(2,128)(2,1)S(1)} %reshape.22), channel_id=1, replica_groups=mesh['groups'=2,'dp'=4,'tensor'=4] {'dp'}, dimensions={0}, use_global_device_ids=true | all-gather | bytes 20480 | tf_op jit(solution)/shard_map/all_gather | solution.py:30
  96.4 0.0 copy-done
  96.4 0.6 fusion.5
  97.1 10.0 %all_to_all.19 = f32[4,2,1024]{2,1,0:T(2,128)S(1)} all-to-all(f32[4,2,1024]{2,1,0:T(2,128)S(1)} %all_to_all.14), channel_id=1, replica_groups=mesh['groups'=2,'dp'=4,'tensor'=4] {'dp'}, dimensions={0} | all-to-all | bytes 65536 | tf_op jit(solution)/shard_map/all_to_all | solution.py:34
  107.1 2.0 copy.14
  109.1 0.0 reduce-scatter.4.cloned.1.call-update
  109.1 0.0 all-gather.6.cloned.1.call-start
  109.1 0.5 all-gather.6.cloned.1.call-update
  109.7 28.5 %reduce-scatter.4.cloned.1.call-done = f32[1024,2]{1,0:T(8,128)} async-done(((f32[4096,2]{1,0:T(8,128)}), f32[1024,2]{1,0:T(8,128)}) %reduce-scatter.4.cloned.1.call-update) | async-done | bytes 8208
  138.1 1.8 copy.15
  140.0 221.0 %all-gather.6.cloned.1.call-done = bf16[1792,4096]{1,0:T(8,128)(2,1)} async-done(((bf16[1792,1024]{1,0:T(8,128)(2,1)}), bf16[1792,4096]{1,0:T(8,128)(2,1)}) %all-gather.6.cloned.1.call-update) | async-done | bytes 14680080 | tf_op jit(solution)/shard_map/all_gather | solution.py:14
  360.9 14.3 %convolution_convert_fusion = bf16[512,1792]{1,0:T(8,128)(2,1)} fusion(bf16[512,4096]{1,0:T(8,128)(2,1)} %all-gather.4.cloned.1.call-done, bf16[1792,4096]{1,0:T(8,128)(2,1)} %all-gather.6.cloned.1.call-done), kind=kOutput, calls=%fused_computation | convolution fusion | flops 7517110272 | bytes 20709376 | tf_op jit(solution)/shard_map/dot_general | solution.py:12
  (3 shorter events, 0.1 us)
Async XLA Ops:
  8.0 88.4 %copy-start = (bf16[1024,1024]{1,0:T(8,128)(2,1)S(1)}, bf16[1024,1024]{1,0:T(8,128)(2,1)}, u32[]{:S(2)}) copy-start(bf16[1024,1024]{1,0:T(8,128)(2,1)} %param.11) | copy-start | bytes 6291460
  8.0 39.6 %copy-start.1 = (bf16[4096,64]{0,1:T(8,128)(2,1)S(1)}, bf16[4096,64]{0,1:T(8,128)(2,1)}, u32[]{:S(2)}) copy-start(bf16[4096,64]{0,1:T(8,128)(2,1)} %param.10) | copy-start | bytes 1572868
  8.0 39.6 %all-gather.4.cloned.1.call-start = ((), (), s32[]{:S(2)}) async-start(), calls=%async_computation.2 | async-start | bytes 5242880 | tf_op jit(solution)/shard_map/all_gather | solution.py:10
  8.8 73.2 %all-reduce.2.cloned.1.call-start = ((), (), s32[]{:S(2)}) async-start(), calls=%async_computation.4 | async-start | bytes 262144 | tf_op jit(solution)/shard_map/psum | solution.py:25
  11.7 126.5 %reduce-scatter.4.cloned.1.call-start = ((), (), s32[]{:S(2)}) async-start(), calls=%async_computation.5 | async-start | bytes 2621440
  109.1 251.8 %all-gather.6.cloned.1.call-start = ((), (), s32[]{:S(2)}) async-start(), calls=%async_computation.3 | async-start | bytes 18350080 | tf_op jit(solution)/shard_map/all_gather | solution.py:14
Sparse Core Ops, SparseCore 0:
  10.4 37.1 all-gather.3
  50.5 31.3 all-reduce.1
  109.2 28.8 reduce-scatter.3
Sparse Core Ops, SparseCore 1:
  111.1 249.7 all-gather.5
where the time goes:
time: 383 us; the launch traced here: 382 us
  waiting for transfers between devices  317 us (83%)
  blocking collectives  23.2 us (6%)
  matrix products  21.8 us (6%)
  between operations  15.2 us (4%)
  local copies, waits for them, and re-layouts  4.62 us (1%)
    all_gather x1, waiting for transfers between devices, local(): lax.all_gather(down_weight, 'dp', axis=1, tiled=True)  221 us
    all_gather x1, waiting for transfers between devices, local(): full_grad = lax.all_gather(out_grad, 'tensor', axis=1, tiled=True)  35.9 us
    psum x1, waiting for transfers between devices, local(): paired = lax.psum(left.reshape(tok_rows // 2, 2 * rank), 'tensor')  30.7 us
    unnamed x5, waiting for transfers between devices  29.7 us
    dot_general x1, matrix products, local(): lax.dot_general(full_grad, lax.all_gather(down_weight, 'dp', axis=1, tile...  14.3 us
    all_gather x1, blocking collectives, local(): everyone = lax.all_gather(features, 'dp', axis=0, tiled=True)  13.2 us
    all_to_all x1, blocking collectives, local(): lax.all_to_all(local_scores, 'dp', split_axis=0, concat_axis=1, tiled=True)  10 us
  transfers between devices with their start and end apart: 4, of which 4 were waited for; matrix products, arithmetic and copies ran while one was open for 2% of the time, Pallas kernels for 0%

commit v1 on v0

v1 whole, which is shorter than its diff:
```python
import functools

import jax
import jax.numpy as jnp
from jax import lax
from jax.experimental import pallas as pl
from jax.experimental.pallas import tpu as pltpu
from jax.sharding import PartitionSpec as P

SEQ = 256
NB = 7
VIA = 2
XC = 2
NT = (((1,), (1,)), ((), ()))


def kernel(n, T, hid, og, w, pin, pout, q, hg, sc,
           wg, xg, obuf, lrbuf, gscr, featbuf, sp, spr,
           loc, xz, xo, xs, wsat, wsend, wr, wy, wv, out,
           lrs, fs_, sps, sprr):
    g, p, t = lax.axis_index("groups"), lax.axis_index("dp"), lax.axis_index("tensor")
    tok, dcols = og.shape
    rows, cw = w.shape
    rb = rows // NB
    hf = rb // 2
    xr = tok // XC
    ex = tok // SEQ
    kk = pin.shape[1]
    nh, U = n // 2, T // 2
    nq, fsz = q.shape
    srows = kk // T
    k = p // 2
    hub_of = lambda pair: 2 * pair + 1 - (4 * pair) // n
    hub = hub_of(k)
    sat = 4 * k + 1 - hub
    u, c = t // 2, lax.rem(t, 2)

    def rc(src, dst, ss, rs, **dev):
        return pltpu.make_async_remote_copy(
            src_ref=src, dst_ref=dst, send_sem=ss, recv_sem=rs,
            device_id=dev, device_id_type=pl.DeviceIdType.MESH)

    def cols(i, width):
        return pl.ds(pl.multiple_of(i * width, width), width)

    def half(b, h):
        return pl.ds(pl.multiple_of(b * rb + h * hf, hf), hf)

    def blk(b):
        return pl.ds(pl.multiple_of(b * rb, rb), rb)

    own_x = pltpu.make_async_copy(og, xg.at[pl.ds(0, tok), cols(t, dcols)], loc.at[0])
    own_w = pltpu.make_async_copy(w, wg.at[:, cols(p, cw)], loc.at[1])
    own_x.start()

    @pl.when(p == hub)
    def _():
        own_w.start()

    bar = pltpu.get_barrier_semaphore()

    @pl.loop(1, n * T)
    def _(i):
        other = lax.rem(p * T + t + i, n * T)
        pl.semaphore_signal(bar, inc=1, device_id={"dp": other // T, "tensor": lax.rem(other, T)},
                            device_id_type=pl.DeviceIdType.MESH)

    pl.semaphore_signal(bar, inc=1, device_id={"groups": 1 - g}, device_id_type=pl.DeviceIdType.MESH)
    pl.semaphore_wait(bar, n * T)

    def sat_x(i):
        return rc(og.at[pl.ds(i * xr, xr), :],
                  xg.at[pl.ds(tok + i * xr, xr), cols(t, dcols)],
                  xz.at[0, i], xz.at[1, i], dp=hub)

    def xrow(a, i):
        return pl.ds(a * tok + i * xr, xr)

    def x_far(a, i, d):
        u2 = lax.rem(u + d, U)
        src = og.at[pl.ds(i * xr, xr), :] if a == 0 else xg.at[xrow(a, i), cols(t, dcols)]
        return rc(src, xg.at[xrow(a, i), cols(t, dcols)],
                  xo.at[0, a, i, d], xo.at[1, a, i, d], tensor=2 * u2 + c)

    def x_mate(a, i, d):
        b = 2 * lax.rem(u + U - d, U) + c
        src = og.at[pl.ds(i * xr, xr), :] if a == 0 and d == 0 else xg.at[xrow(a, i), cols(b, dcols)]
        return rc(src, xg.at[xrow(a, i), cols(b, dcols)],
                  xs.at[0, a, i, d], xs.at[1, a, i, d], tensor=2 * u + 1 - c)

    def sat_w(b, o):
        h = g if o == 0 else 1 - g
        return rc(w.at[half(b, h), :], wg.at[half(b, h), cols(sat, cw)],
                  wsend.at[o, b], wsat.at[o, b], dp=hub)

    def hub_w(b, r, s):
        to = hub_of(lax.rem(k + r, nh))
        src = w.at[half(b, g), :] if s == 0 else wg.at[half(b, g), cols(sat, cw)]
        dst = wg.at[half(b, g), cols(p if s == 0 else sat, cw)]
        return rc(src, dst, wr.at[0, s, b, r], wr.at[1, s, b, r], dp=to)

    def y_w(b, r, s):
        k2 = lax.rem(k + nh - r, nh)
        h2 = hub_of(k2)
        at = wg.at[half(b, g), cols(h2 if s == 0 else 4 * k2 + 1 - h2, cw)]
        return rc(at, at, wy.at[0, s, b, r], wy.at[1, s, b, r], groups=1 - g)

    def y_sat(b):
        at = wg.at[half(b, g), cols(sat, cw)]
        return rc(at, at, wv.at[0, b], wv.at[1, b], groups=1 - g)

    def ret(b):
        return rc(obuf.at[:, cols(b, rb)], hg.at[:, cols(b, rb)],
                  out.at[0, b], out.at[1, b], dp=sat)

    def lr_copy(d):
        return rc(lrbuf.at[t], lrbuf.at[t], lrs.at[0, d], lrs.at[1, d],
                  tensor=lax.rem(t + d, T))

    def f_copy(d):
        return rc(featbuf.at[p], featbuf.at[p], fs_.at[0, d], fs_.at[1, d],
                  dp=lax.rem(p + d, n))

    bpt = n // T
    t_to, slot = p // bpt, lax.rem(p, bpt) * T + t

    def s_copy(d):
        p2 = lax.rem(p + d, n)
        return rc(sp.at[p2], spr.at[slot], sps.at[d], sprr.at[slot], dp=p2, tensor=t_to)

    def left_right():
        own_x.wait()
        left = jnp.dot(hid[...], pin[...], preferred_element_type=jnp.float32)
        right = jnp.dot(xg[pl.ds(0, tok), cols(t, dcols)], pout[cols(t, dcols), :],
                        preferred_element_type=jnp.float32)
        lrbuf[t] = jnp.concatenate([left, right], axis=1)
        for d in range(1, T):
            lr_copy(d).start()

    def features():
        for d in range(1, T):
            lr_copy(d).wait_recv()
        R = featbuf.shape[1]
        row = lax.broadcasted_iota(jnp.int32, (R, 2 * kk), 0)
        lane = lax.broadcasted_iota(jnp.int32, (1, 2 * kk), 1)
        for e in range(ex):
            lr = lrbuf[0, pl.ds(e * SEQ, SEQ), :]
            for s in range(1, T):
                lr = lr + lrbuf[s, pl.ds(e * SEQ, SEQ), :]
            right = lr[:, kk:]
            gscr[e] = jnp.dot(lr.T, jnp.concatenate([right, right], axis=1),
                              precision=lax.Precision.HIGHEST,
                              preferred_element_type=jnp.float32)
        mine = [gscr[e, pl.ds(pl.multiple_of(t * srows, srows), srows), :] for e in range(ex)]
        for j in range(srows // 2):
            val = jnp.zeros((R, 2 * kk), jnp.float32)
            for e in range(ex):
                vec = jnp.where(lane < kk, mine[e][2 * j:2 * j + 1], mine[e][2 * j + 1:2 * j + 2])
                val = jnp.where(row == p * ex + e, vec, val)
            featbuf[p, :, pl.ds(j * 2 * kk, 2 * kk)] = val.astype(jnp.bfloat16)
        for d in range(1, n):
            f_copy(d).start()

    def partial_scores():
        for d in range(1, n):
            f_copy(d).wait_recv()
        every = featbuf[0].astype(jnp.float32)
        for s in range(1, n):
            every = every + featbuf[s].astype(jnp.float32)
        s = lax.dot_general(every.astype(jnp.bfloat16), q[...], NT, preferred_element_type=jnp.float32)
        sp[...] = jnp.zeros_like(sp)
        for i in range(n):
            sp[i, 0:ex, :] = s[i * ex:(i + 1) * ex]
        for d in range(1, n):
            s_copy(d).start()

        @pl.when(t_to == t)
        def _():
            spr[slot] = sp[p]

        @pl.when(t_to != t)
        def _():
            s_copy(0).start()

    def finish_scores():
        for i in range(bpt * T):
            me = jnp.logical_and(t * bpt + i // T == p, i % T == t)

            @pl.when(jnp.logical_not(me))
            def _():
                rc(sp.at[0], spr.at[i], sps.at[0], sprr.at[i], dp=p, tensor=t).wait_recv()

        for b in range(bpt):
            tot = spr[b * T, 0:ex, :]
            for s in range(1, T):
                tot = tot + spr[b * T + s, 0:ex, :]
            sc[:, pl.ds(b * nq, nq)] = tot

    @pl.when(p != hub)
    def _():
        for i in range(XC):
            sat_x(i).start()
        order = [(b, 0) for b in range(VIA)]
        for b in range(VIA, NB):
            order.append((b, 0))
            if b > VIA:
                order.append((b - 1, 1))
        order.append((NB - 1, 1))
        for b, o in order:
            sat_w(b, o).start()
        left_right()
        features()
        partial_scores()
        finish_scores()
        for b in range(NB):
            ret(b).wait_recv()
        for i in range(XC):
            sat_x(i).wait_send()
        for b, o in order:
            sat_w(b, o).wait_send()

    @pl.when(p == hub)
    def _():
        for i in range(XC):
            for d in range(1, U):
                x_far(0, i, d).start()
            x_mate(0, i, 0).start()

        @pl.loop(0, NB)
        def _(b):
            @pl.loop(1, nh)
            def _(r):
                hub_w(b, r, 0).start()

        left_right()

        def pass_own(lo, hi):
            @pl.loop(lo, hi)
            def _(b):
                @pl.loop(1, nh)
                def _(r):
                    hub_w(b, r, 0).wait_recv()
                    y_w(b, r, 0).start()

        def pass_x(a, i):
            for d in range(1, U):
                x_far(a, i, d).wait_recv()
                x_mate(a, i, d).start()

        def take_sat(i):
            sat_x(i).wait_recv()
            for d in range(1, U):
                x_far(1, i, d).start()
            x_mate(1, i, 0).start()

        for i in range(XC):
            pass_own(2 * i, 2 * i + 2)
            pass_x(0, i)
            take_sat(i)
        pass_own(2 * XC, NB)
        features()
        pass_x(1, 0)

        @pl.loop(0, NB + 2)
        def _(s):
            @pl.when(s < NB)
            def _():
                sat_w(s, 0).wait_recv()

                @pl.loop(1, nh)
                def _(r):
                    hub_w(s, r, 1).start()

                @pl.when(s < VIA)
                def _():
                    y_sat(s).start()

            @pl.when(jnp.logical_and(s >= 1, s <= NB))
            def _():
                @pl.loop(1, nh)
                def _(r):
                    hub_w(s - 1, r, 1).wait_recv()
                    y_w(s - 1, r, 1).start()

            @pl.when(s == 1)
            def _():
                for i in range(1, XC):
                    pass_x(1, i)
                partial_scores()
                own_w.wait()
                for a in range(2):
                    for i in range(XC):
                        for d in range(U):
                            x_mate(a, i, d).wait_recv()

            @pl.when(s == 3)
            def _():
                finish_scores()

            @pl.when(s >= 2)
            def _():
                b = s - 2

                @pl.loop(1, nh)
                def _(r):
                    for j in range(2):
                        y_w(b, r, j).wait_recv()

                @pl.when(b < VIA)
                def _():
                    y_sat(b).wait_recv()

                @pl.when(b >= VIA)
                def _():
                    sat_w(b, 1).wait_recv()

                @pl.loop(0, tok // SEQ)
                def _(m):
                    at = pl.ds(pl.multiple_of(m * SEQ, SEQ), SEQ)
                    x = xg[pl.ds(pl.multiple_of(tok + m * SEQ, SEQ), SEQ), :]
                    obuf[at, cols(b, rb)] = lax.dot_general(
                        x, wg[blk(b), :], NT, preferred_element_type=jnp.float32
                    ).astype(jnp.bfloat16)

                ret(b).start()

                @pl.loop(0, tok // SEQ)
                def _(m):
                    at = pl.ds(pl.multiple_of(m * SEQ, SEQ), SEQ)
                    hg[at, cols(b, rb)] = lax.dot_general(
                        xg[at, :], wg[blk(b), :], NT, preferred_element_type=jnp.float32
                    ).astype(jnp.bfloat16)

        for a in range(2):
            for i in range(XC):
                for d in range(1, U):
                    x_far(a, i, d).wait_send()
                for d in range(U):
                    x_mate(a, i, d).wait_send()

        @pl.loop(0, NB)
        def _(b):
            @pl.loop(1, nh)
            def _(r):
                for s in range(2):
                    hub_w(b, r, s).wait_send()
                    y_w(b, r, s).wait_send()

            @pl.when(b < VIA)
            def _():
                y_sat(b).wait_send()

            ret(b).wait_send()

    for d in range(1, T):
        lr_copy(d).wait_send()
    for d in range(1, n):
        f_copy(d).wait_send()
        s_copy(d).wait_send()

    @pl.when(t_to != t)
    def _():
        s_copy(0).wait_send()


def local(n, T, hidden, out_grad, down_weight, proj_in, proj_out, queries):
    tok, dcols = out_grad.shape
    rows, cw = down_weight.shape
    kk = proj_in.shape[1]
    ex = tok // SEQ
    nq, fsz = queries.shape
    R = -(-n * ex // 16) * 16
    nh, U = n // 2, T // 2
    bf, f32 = jnp.bfloat16, jnp.float32
    vm, hb = pl.BlockSpec(memory_space=pltpu.VMEM), pl.BlockSpec(memory_space=pl.ANY)
    dma = pltpu.SemaphoreType.DMA
    return pl.pallas_call(
        functools.partial(kernel, n, T),
        out_shape=(jax.ShapeDtypeStruct((tok, rows), bf),
                   jax.ShapeDtypeStruct((ex, nq * n // T), f32)),
        in_specs=[vm, hb, hb, vm, vm, vm],
        out_specs=(vm, vm),
        scratch_shapes=[
            pltpu.VMEM((rows, cw * n), bf),
            pltpu.VMEM((2 * tok, dcols * T), bf),
            pltpu.VMEM((tok, rows), bf),
            pltpu.VMEM((T, tok, 2 * kk), f32),
            pltpu.VMEM((ex, 2 * kk, 2 * kk), f32),
            pltpu.VMEM((n, R, fsz), bf),
            pltpu.VMEM((n, 8, nq), f32),
            pltpu.VMEM((n // T * T, 8, nq), f32),
            dma((2,)),
            dma((2, XC)),
            dma((2, 2, XC, U)),
            dma((2, 2, XC, U)),
            dma((2, NB)),
            dma((2, NB)),
            dma((2, 2, NB, nh)),
            dma((2, 2, NB, nh)),
            dma((2, NB)),
            dma((2, NB)),
            dma((2, T)),
            dma((2, n)),
            dma((n,)),
            dma((n // T * T,)),
        ],
        compiler_params=pltpu.CompilerParams(
            collective_id=0, has_side_effects=True, vmem_limit_bytes=56 * 2**20),
        cost_estimate=pl.CostEstimate(flops=4 * tok * rows * cw * n, bytes_accessed=2 * rows * cw * n,
                                      transcendentals=0),
    )(hidden, out_grad, down_weight, proj_in, proj_out, queries)


def solution(mesh):
    in_specs = (
        P(("groups", "dp"), "tensor"),
        P(("groups", "dp"), "tensor"),
        P("tensor", "dp"),
        P("tensor", None),
        P(),
        P("dp", "tensor"),
    )
    out_specs = (P(("groups", "dp"), "tensor"), P(("groups", "dp"), "tensor"))
    body = functools.partial(local, mesh.shape["dp"], mesh.shape["tensor"])
    return jax.shard_map(body, mesh=mesh, in_specs=in_specs, out_specs=out_specs, check_vma=False)
```

time: 383 us -> 163 us (0.43)
  waiting for transfers between devices: 317 us -> 0 us
  Pallas kernels: 0 us -> 154 us
  blocking collectives: 23.2 us -> 0 us
  matrix products: 21.8 us -> 0 us
  between operations: 15.2 us -> 0.65 us
    all_gather x2 -> x0, waiting for transfers between devices: 257 us -> none  [the longest x1 221 us: local(): lax.all_gather(down_weight, 'dp', axis=1, tiled=True)]
    pallas_call x0 -> x1, Pallas kernels: none -> 154 us  [local(): pl.pallas_call(functools.partial(kernel, n, T), out_shape=(jax.ShapeDtype...]
    psum x1 -> x0, waiting for transfers between devices: 30.7 us -> none  [local(): paired = lax.psum(left.reshape(tok_rows // 2, 2 * rank), 'tensor')]
    unnamed x5 -> x0, waiting for transfers between devices: 29.7 us -> none
    dot_general x5 -> x0, matrix products: 21.8 us -> none  [the longest x1 14.3 us: local(): lax.dot_general(full_grad, lax.all_gather(down_weight, 'dp', axis=1, tile...]
    all_gather x1 -> x0, blocking collectives: 13.2 us -> none  [local(): everyone = lax.all_gather(features, 'dp', axis=0, tiled=True)]
    all_to_all x1 -> x0, blocking collectives: 10 us -> none  [local(): lax.all_to_all(local_scores, 'dp', split_axis=0, concat_axis=1, tiled=True)]
    unnamed x8 -> x6, local copies, waits for them, and re-layouts: 3.9 us -> 7.74 us
  transfers between devices with their start and end apart: 4 -> 0, of which waited for: 4 -> 0; matrix products, arithmetic and copies ran while one was open for 2% -> 0% of each run, Pallas kernels for 0% -> 0%
where the time goes in v1:
time: 163 us
  Pallas kernels  154 us (94%)
  local copies, waits for them, and re-layouts  7.74 us (5%)
    pallas_call x1, Pallas kernels, local(): pl.pallas_call(functools.partial(kernel, n, T), out_shape=(jax.ShapeDtype...  154 us
    unnamed x6, local copies, waits for them, and re-layouts  7.74 us

profile of v1, /device:TPU:0, one launch (start us, length us, event | category | flops | bytes accessed | tf_op | source)
XLA Modules:
  0.0 162.7 jit_solution(4711078547187332154)
XLA Ops:
  0.6 1.9 %copy.8.pin = bf16[1792,64]{1,0:T(8,128)(2,1)} copy(bf16[1792,64]{0,1:T(8,128)(2,1)} %param.9) | data formatting | bytes 458752 | tf_op args[3]
  2.6 2.4 %copy.9.pout = bf16[4096,64]{1,0:T(8,128)(2,1)} copy(bf16[4096,64]{0,1:T(8,128)(2,1)} %param.10) | data formatting | bytes 1048576 | tf_op args[4]
  4.9 154.3 %shard_map.77 = (bf16[512,1792]{1,0:T(8,128)(2,1)}, f32[2,1024]{1,0:T(2,128)}) custom-call(bf16[512,1792]{1,0:T(8,128)(2,1)} %hid.1, bf16[512,1024]{1,0:T(8,128)(2,1)} %og.1, bf16[1792,1024]{1,0:T(8,128)(2,1)} %w.1, bf16[1792,64]{1,0:T(8,128)(2,1)} %copy.8.pin, bf16[4096,64]{1,0:T(8,128)(2,1)} %copy.9.pout, bf16[1024,1024]{1,0:T(8,128)(2,1)} %q.1), custom_call_target="tpu_custom_call" | custom-call | flops 15032385536 | bytes 14680064 | tf_op jit(solution)/shard_map/pallas_call | solution.py:377
  159.3 0.0 copy-start
  159.3 2.9 %copy.12 = bf16[512,1792]{1,0:T(8,128)(2,1)} copy(bf16[512,1792]{1,0:T(8,128)(2,1)} %get-tuple-element.4) | data formatting | bytes 3670016
  162.1 0.0 copy-done
  162.1 0.6 copy.13
Async XLA Ops:
  159.3 2.9 %copy-start = (f32[2,1024]{1,0:T(2,128)S(1)}, f32[2,1024]{1,0:T(2,128)}, u32[]{:S(2)}) copy-start(f32[2,1024]{1,0:T(2,128)} %get-tuple-element.5) | copy-start | bytes 24580

commit v2 on v1

--- a/solution.py
+++ b/solution.py
@@ -10,7 +10,8 @@
 SEQ = 256
 NB = 7
 VIA = 2
-XC = 2
+XC = 4
+WIN = 3
 NT = (((1,), (1,)), ((), ()))
 
 
@@ -25,7 +26,7 @@
     hf = rb // 2
     xr = tok // XC
     ex = tok // SEQ
-    kk = pin.shape[1]
+    kk = pin.shape[0]
     nh, U = n // 2, T // 2
     nq, fsz = q.shape
     srows = kk // T
@@ -130,9 +131,9 @@
 
     def left_right():
         own_x.wait()
-        left = jnp.dot(hid[...], pin[...], preferred_element_type=jnp.float32)
-        right = jnp.dot(xg[pl.ds(0, tok), cols(t, dcols)], pout[cols(t, dcols), :],
-                        preferred_element_type=jnp.float32)
+        left = lax.dot_general(hid[...], pin[...], NT, preferred_element_type=jnp.float32)
+        right = lax.dot_general(xg[pl.ds(0, tok), cols(t, dcols)], pout[:, cols(t, dcols)], NT,
+                                preferred_element_type=jnp.float32)
         lrbuf[t] = jnp.concatenate([left, right], axis=1)
         for d in range(1, T):
             lr_copy(d).start()
@@ -198,26 +199,28 @@
 
     @pl.when(p != hub)
     def _():
-        for i in range(XC):
-            sat_x(i).start()
         order = [(b, 0) for b in range(VIA)]
         for b in range(VIA, NB):
             order.append((b, 0))
             if b > VIA:
                 order.append((b - 1, 1))
         order.append((NB - 1, 1))
-        for b, o in order:
-            sat_w(b, o).start()
-        left_right()
-        features()
-        partial_scores()
+        sends = [sat_x(i) for i in range(XC)] + [sat_w(b, o) for b, o in order]
+        for i, copy in enumerate(sends):
+            if i >= WIN:
+                sends[i - WIN].wait_send()
+            copy.start()
+            if i == WIN - 1:
+                left_right()
+            elif i == XC + 3:
+                features()
+            elif i == XC + 8:
+                partial_scores()
+        for copy in sends[-WIN:]:
+            copy.wait_send()
         finish_scores()
         for b in range(NB):
             ret(b).wait_recv()
-        for i in range(XC):
-            sat_x(i).wait_send()
-        for b, o in order:
-            sat_w(b, o).wait_send()
 
     @pl.when(p == hub)
     def _():
@@ -254,10 +257,9 @@
             x_mate(1, i, 0).start()
 
         for i in range(XC):
-            pass_own(2 * i, 2 * i + 2)
+            pass_own(NB * i // XC, NB * (i + 1) // XC)
             pass_x(0, i)
             take_sat(i)
-        pass_own(2 * XC, NB)
         features()
         pass_x(1, 0)
 
@@ -282,9 +284,14 @@
                     hub_w(s - 1, r, 1).wait_recv()
                     y_w(s - 1, r, 1).start()
 
+            @pl.when(s == 0)
+            def _():
+                for i in range(1, XC // 2):
+                    pass_x(1, i)
+
             @pl.when(s == 1)
             def _():
-                for i in range(1, XC):
+                for i in range(XC // 2, XC):
                     pass_x(1, i)
                 partial_scores()
                 own_w.wait()
@@ -408,7 +415,7 @@
             collective_id=0, has_side_effects=True, vmem_limit_bytes=56 * 2**20),
         cost_estimate=pl.CostEstimate(flops=4 * tok * rows * cw * n, bytes_accessed=2 * rows * cw * n,
                                       transcendentals=0),
-    )(hidden, out_grad, down_weight, proj_in, proj_out, queries)
+    )(hidden, out_grad, down_weight, proj_in.T, proj_out.T, queries)
 
 
 def solution(mesh):

time: 163 us -> 130 us (0.80)
  Pallas kernels: 154 us -> 126 us
  local copies, waits for them, and re-layouts: 7.74 us -> 3.45 us
    pallas_call x1, Pallas kernels: 154 us -> 126 us  [local(): pl.pallas_call(functools.partial(kernel, n, T), out_shape=(jax.ShapeDtype...]
    unnamed x6 -> x4, local copies, waits for them, and re-layouts: 7.74 us -> 3.45 us
where the time goes in v2:
time: 130 us
  Pallas kernels  126 us (97%)
  local copies, waits for them, and re-layouts  3.45 us (3%)
    pallas_call x1, Pallas kernels, local(): pl.pallas_call(functools.partial(kernel, n, T), out_shape=(jax.ShapeDtype...  126 us
    unnamed x4, local copies, waits for them, and re-layouts  3.45 us

profile of v2, /device:TPU:0, one launch (start us, length us, event | category | flops | bytes accessed | tf_op | source)
XLA Modules:
  0.0 129.8 jit_solution(14922188056136799467)
XLA Ops:
  0.6 125.7 %shard_map.77 = (bf16[512,1792]{1,0:T(8,128)(2,1)}, f32[2,1024]{1,0:T(2,128)}) custom-call(bf16[512,1792]{1,0:T(8,128)(2,1)} %hid.1, bf16[512,1024]{1,0:T(8,128)(2,1)} %og.1, bf16[1792,1024]{1,0:T(8,128)(2,1)} %w.1, bf16[64,1792]{1,0:T(8,128)(2,1)} %bitcast.3, bf16[64,4096]{1,0:T(8,128)(2,1)} %bitcast.2, bf16[1024,1024]{1,0:T(8,128)(2,1)} %q.1), custom_call_target="tpu_custom_call" | custom-call | flops 15032385536 | bytes 14680064 | tf_op jit(solution)/shard_map/pallas_call | solution.py:384
  126.3 0.0 copy-start
  126.3 2.9 %copy.10 = bf16[512,1792]{1,0:T(8,128)(2,1)} copy(bf16[512,1792]{1,0:T(8,128)(2,1)} %get-tuple-element.4) | data formatting | bytes 3670016
  129.2 0.0 copy-done
  129.2 0.6 copy.11
Async XLA Ops:
  126.3 2.9 %copy-start = (f32[2,1024]{1,0:T(2,128)S(1)}, f32[2,1024]{1,0:T(2,128)}, u32[]{:S(2)}) copy-start(f32[2,1024]{1,0:T(2,128)} %get-tuple-element.5) | copy-start | bytes 24580

commit v3 on v2

--- a/solution.py
+++ b/solution.py
@@ -11,11 +11,13 @@
 NB = 7
 VIA = 2
 XC = 4
+LAG = 3
 WIN = 3
 NT = (((1,), (1,)), ((), ()))
 
 
-def kernel(n, T, hid, og, w, pin, pout, q, hg, sc,
+def kernel(n, T, hid_in, og, w, pin, pout, q_in, hg, sc,
+           hid, q,
            wg, xg, obuf, lrbuf, gscr, featbuf, sp, spr,
            loc, xz, xo, xs, wsat, wsend, wr, wy, wv, out,
            lrs, fs_, sps, sprr):
@@ -52,7 +54,11 @@
 
     own_x = pltpu.make_async_copy(og, xg.at[pl.ds(0, tok), cols(t, dcols)], loc.at[0])
     own_w = pltpu.make_async_copy(w, wg.at[:, cols(p, cw)], loc.at[1])
+    get_hid = pltpu.make_async_copy(hid_in, hid, loc.at[2])
+    get_q = pltpu.make_async_copy(q_in, q, loc.at[3])
     own_x.start()
+    get_hid.start()
+    get_q.start()
 
     @pl.when(p == hub)
     def _():
@@ -131,6 +137,7 @@
 
     def left_right():
         own_x.wait()
+        get_hid.wait()
         left = lax.dot_general(hid[...], pin[...], NT, preferred_element_type=jnp.float32)
         right = lax.dot_general(xg[pl.ds(0, tok), cols(t, dcols)], pout[:, cols(t, dcols)], NT,
                                 preferred_element_type=jnp.float32)
@@ -163,6 +170,7 @@
             f_copy(d).start()
 
     def partial_scores():
+        get_q.wait()
         for d in range(1, n):
             f_copy(d).wait_recv()
         every = featbuf[0].astype(jnp.float32)
@@ -214,10 +222,9 @@
                 left_right()
             elif i == XC + 3:
                 features()
-            elif i == XC + 8:
-                partial_scores()
         for copy in sends[-WIN:]:
             copy.wait_send()
+        partial_scores()
         finish_scores()
         for b in range(NB):
             ret(b).wait_recv()
@@ -234,8 +241,6 @@
             @pl.loop(1, nh)
             def _(r):
                 hub_w(b, r, 0).start()
-
-        left_right()
 
         def pass_own(lo, hi):
             @pl.loop(lo, hi)
@@ -260,10 +265,9 @@
             pass_own(NB * i // XC, NB * (i + 1) // XC)
             pass_x(0, i)
             take_sat(i)
-        features()
-        pass_x(1, 0)
-
-        @pl.loop(0, NB + 2)
+        left_right()
+
+        @pl.loop(0, NB + LAG)
         def _(s):
             @pl.when(s < NB)
             def _():
@@ -284,29 +288,22 @@
                     hub_w(s - 1, r, 1).wait_recv()
                     y_w(s - 1, r, 1).start()
 
-            @pl.when(s == 0)
-            def _():
-                for i in range(1, XC // 2):
+            for i in range(XC):
+                @pl.when(s == i)
+                def _():
                     pass_x(1, i)
 
-            @pl.when(s == 1)
-            def _():
-                for i in range(XC // 2, XC):
-                    pass_x(1, i)
-                partial_scores()
+            @pl.when(s == LAG)
+            def _():
                 own_w.wait()
                 for a in range(2):
                     for i in range(XC):
                         for d in range(U):
                             x_mate(a, i, d).wait_recv()
 
-            @pl.when(s == 3)
-            def _():
-                finish_scores()
-
-            @pl.when(s >= 2)
-            def _():
-                b = s - 2
+            @pl.when(s >= LAG)
+            def _():
+                b = s - LAG
 
                 @pl.loop(1, nh)
                 def _(r):
@@ -337,6 +334,16 @@
                     hg[at, cols(b, rb)] = lax.dot_general(
                         xg[at, :], wg[blk(b), :], NT, preferred_element_type=jnp.float32
                     ).astype(jnp.bfloat16)
+
+            @pl.when(s == LAG + 1)
+            def _():
+                features()
+
+            @pl.when(s == NB - 1)
+            def _():
+                partial_scores()
+
+        finish_scores()
 
         for a in range(2):
             for i in range(XC):
@@ -385,9 +392,11 @@
         functools.partial(kernel, n, T),
         out_shape=(jax.ShapeDtypeStruct((tok, rows), bf),
                    jax.ShapeDtypeStruct((ex, nq * n // T), f32)),
-        in_specs=[vm, hb, hb, vm, vm, vm],
+        in_specs=[hb, hb, hb, vm, vm, hb],
         out_specs=(vm, vm),
         scratch_shapes=[
+            pltpu.VMEM(hidden.shape, bf),
+            pltpu.VMEM(queries.shape, bf),
             pltpu.VMEM((rows, cw * n), bf),
             pltpu.VMEM((2 * tok, dcols * T), bf),
             pltpu.VMEM((tok, rows), bf),
@@ -396,7 +405,7 @@
             pltpu.VMEM((n, R, fsz), bf),
             pltpu.VMEM((n, 8, nq), f32),
             pltpu.VMEM((n // T * T, 8, nq), f32),
-            dma((2,)),
+            dma((4,)),
             dma((2, XC)),
             dma((2, 2, XC, U)),
             dma((2, 2, XC, U)),

time: 130 us -> 126 us (0.969)
  Pallas kernels: 126 us -> 121 us
    pallas_call x1, Pallas kernels: 126 us -> 121 us  [local(): pl.pallas_call(functools.partial(kernel, n, T), out_shape=(jax.ShapeDtype...]
where the time goes in v3:
time: 126 us
  Pallas kernels  121 us (96%)
  local copies, waits for them, and re-layouts  3.45 us (3%)
    pallas_call x1, Pallas kernels, local(): pl.pallas_call(functools.partial(kernel, n, T), out_shape=(jax.ShapeDtype...  121 us
    unnamed x4, local copies, waits for them, and re-layouts  3.45 us

profile of v3, /device:TPU:0, one launch (start us, length us, event | category | flops | bytes accessed | tf_op | source)
XLA Modules:
  0.0 125.6 jit_solution(4254655798613511791)
XLA Ops:
  0.6 121.5 %shard_map.77 = (bf16[512,1792]{1,0:T(8,128)(2,1)}, f32[2,1024]{1,0:T(2,128)}) custom-call(bf16[512,1792]{1,0:T(8,128)(2,1)} %hid_in.1, bf16[512,1024]{1,0:T(8,128)(2,1)} %og.1, bf16[1792,1024]{1,0:T(8,128)(2,1)} %w.1, bf16[64,1792]{1,0:T(8,128)(2,1)} %bitcast.3, bf16[64,4096]{1,0:T(8,128)(2,1)} %bitcast.2, bf16[1024,1024]{1,0:T(8,128)(2,1)} %q_in.1), custom_call_target="tpu_custom_call" | custom-call | flops 15032385536 | bytes 14680064 | tf_op jit(solution)/shard_map/pallas_call | solution.py:391
  122.1 0.0 copy-start
  122.1 2.9 %copy.10 = bf16[512,1792]{1,0:T(8,128)(2,1)} copy(bf16[512,1792]{1,0:T(8,128)(2,1)} %get-tuple-element.4) | data formatting | bytes 3670016
  125.0 0.0 copy-done
  125.0 0.6 copy.11
Async XLA Ops:
  122.1 2.9 %copy-start = (f32[2,1024]{1,0:T(2,128)S(1)}, f32[2,1024]{1,0:T(2,128)}, u32[]{:S(2)}) copy-start(f32[2,1024]{1,0:T(2,128)} %get-tuple-element.5) | copy-start | bytes 24580
